TPU v7x, 512 devices: a whole 4x4x16 slice. The times are simulated.
512 devices in a mesh: off: 32 (over x_lo, z), rows: 16 (over x_hi, y, core).
Axes of the slice: x: 4 (x_hi: 2, x_lo: 2; x = x_hi * 2 + x_lo), y: 4, z: 16, core: 2. Of those that a mesh axis runs over, the one named last changes fastest.
Arguments:
- volume: bfloat16 [256, 16, 64, 480], P('off', None, 'rows'), may hold values from -6 to 6
- offset_kernels: bfloat16 [2, 9, 16, 16], replicated, may hold values from -0.75 to 0.75
- offset_biases: float32 [2, 16], replicated, may hold values from -3 to 3
- spatial_kernels: bfloat16 [2, 9, 16, 16], replicated, may hold values from -0.75 to 0.75
- spatial_biases: float32 [2, 16], replicated, may hold values from -3 to 3
Outputs:
- filtered: bfloat16 [256, 16, 64, 480], P('off', None, 'rows')
All inputs are finite; a program needn't handle non-finite values.
Results may differ from a plain program's by a relative error of at most 0.0058.
Values may be sent and summed in bfloat16 or wider, within the bound.
A program may use at most 64 MiB of HBM per device.

v0:
```python
import jax
import jax.numpy as jnp
from jax import lax
from jax.sharding import PartitionSpec as P

U = 16
CH = 16
ROUNDS = 2


def with_halo(cells, sides, width):
    for axis, dim in sides:
        count = lax.axis_size(axis)
        ends = count - 1
        head = lax.slice_in_dim(cells, 0, width, axis=dim)
        tail = lax.slice_in_dim(cells, cells.shape[dim] - width, cells.shape[dim], axis=dim)
        cells = jnp.concatenate(
            [
                lax.ppermute(tail, axis, [(i, (i + 1) % count) for i in range(ends)]),
                cells,
                lax.ppermute(head, axis, [((i + 1) % count, i) for i in range(ends)]),
            ],
            axis=dim,
        )
    return cells


def offset_mix(received, kernel, biases):
    count = received.shape[3]
    grid_view = received.reshape(U, U, CH, count)
    padded = jnp.pad(grid_view, ((1, 1), (1, 1), (0, 0), (0, 0)))
    stacked = jnp.stack([padded[a : a + U, b : b + U] for a in range(3) for b in range(3)], 0)
    summed = jnp.einsum("tkc,tuvcp->uvkp", kernel, stacked, preferred_element_type=jnp.float32)
    result = jax.nn.relu(summed + biases[:, None]).astype(jnp.bfloat16)
    return result.reshape(U * U, CH, 1, count)


def swapped_mix(volume, kernel, biases):
    groups = lax.axis_size("off")
    own_count, channels, rows_here, width = volume.shape
    piece_length = rows_here * width // groups
    split_view = volume.reshape(own_count, channels, groups, piece_length)
    mixed = offset_mix(
        lax.all_to_all(split_view, "off", split_axis=2, concat_axis=0, tiled=True), kernel, biases
    )
    result = lax.all_to_all(mixed, "off", split_axis=0, concat_axis=2, tiled=True)
    return result.reshape(own_count, channels, rows_here, width)


def spatial_mix(volume, kernel, biases):
    rows_here = volume.shape[2]
    width = volume.shape[3]
    extended = with_halo(volume, (("rows", 2),), 1)
    padded = jnp.pad(extended, ((0, 0), (0, 0), (0, 0), (1, 1)))
    stacked = jnp.stack(
        [padded[:, :, a : a + rows_here, b : b + width] for a in range(3) for b in range(3)], 0
    )
    summed = jnp.einsum("tkc,tocrw->okrw", kernel, stacked, preferred_element_type=jnp.float32)
    return jax.nn.relu(summed + biases[None, :, None, None]).astype(jnp.bfloat16)


def local(volume, offset_kernels, offset_biases, spatial_kernels, spatial_biases):
    current = volume
    for round_number in range(ROUNDS):
        current = swapped_mix(current, offset_kernels[round_number], offset_biases[round_number])
        current = spatial_mix(current, spatial_kernels[round_number], spatial_biases[round_number])
    return current


def solution(mesh):
    in_specs = (P("off", None, "rows", None), P(), P(), P(), P())
    out_specs = P("off", None, "rows", None)
    return jax.shard_map(local, mesh=mesh, in_specs=in_specs, out_specs=out_specs, check_vma=False)
```

profile of v0, /device:TPU:57, one launch (start us, length us, event | category | flops | bytes accessed | tf_op | source)
XLA Modules:
  0.0 226.6 jit_solution(15589591485237791254)
XLA Ops:
  0.0 2.1 reshape.36
  2.6 3.6 %reshape.52 = bf16[32,2,3840]{2,1,0:T(2,128)(2,1)} reshape(bf16[32,8,16,60]{3,2,1,0:T(8,128)(2,1)S(1)} %bitcast.332) | data formatting | bytes 983040
  6.1 16.1 %all-to-all-start = ((bf16[32,2,3840]{2,1,0:T(2,128)(2,1)}), bf16[32,2,3840]{2,1,0:T(2,128)(2,1)S(1)}, u32[]{:S(2)}, u32[]{:S(2)}) async-start(bf16[32,2,3840]{2,1,0:T(2,128)(2,1)} %reshape.52), calls=%async_computation | async-start | bytes 983040 | tf_op jit(solution)/shard_map/all_to_all | solution.py:44
  22.3 29.4 %all-to-all-done = bf16[32,2,3840]{2,1,0:T(2,128)(2,1)S(1)} async-done(((bf16[32,2,3840]{2,1,0:T(2,128)(2,1)}), bf16[32,2,3840]{2,1,0:T(2,128)(2,1)S(1)}, u32[]{:S(2)}, u32[]{:S(2)}) %all-to-all-start) | async-done | bytes 491552 | tf_op jit(solution)/shard_map/all_to_all | solution.py:44
  51.7 3.5 %reshape.53 = bf16[32,8,16,60]{3,2,1,0:T(8,128)(2,1)S(1)} reshape(bf16[32,2,3840]{2,1,0:T(2,128)(2,1)S(1)} %all-to-all-done) | data formatting | bytes 983040
  58.2 1.4 fusion.3
  59.6 2.8 %reshape.54 = bf16[32,2,3840]{2,1,0:T(2,128)(2,1)S(1)} reshape(bf16[256,1,16,60]{3,2,1,0:T(8,128)(2,1)S(1)} %bitcast.336) | data formatting | bytes 983040
  62.4 35.5 %all_to_all.60 = bf16[32,2,3840]{2,1,0:T(2,128)(2,1)S(1)} all-to-all(bf16[32,2,3840]{2,1,0:T(2,128)(2,1)S(1)} %reshape.54), channel_id=1, replica_groups=mesh['off'=32,'rows'=16] {'off'}, dimensions={0} | all-to-all | bytes 983040 | tf_op jit(solution)/shard_map/all_to_all | solution.py:46
  97.9 3.5 %reshape.55 = bf16[256,1,16,60]{3,2,1,0:T(8,128)(2,1)S(1)} reshape(bf16[32,2,3840]{2,1,0:T(2,128)(2,1)S(1)} %all_to_all.60) | data formatting | bytes 983040
  101.4 0.7 copy.131
  102.1 0.9 reshape.39
  103.2 6.5 %collective-permute-start = (bf16[8,16,1,480]{3,1,2,0:T(8,128)(2,1)S(1)}, bf16[8,16,1,480]{3,1,2,0:T(8,128)(2,1)S(1)}, u32[]{:S(2)}, u32[]{:S(2)}) collective-permute-start(bf16[8,16,1,480]{3,1,2,0:T(8,128)(2,1)S(1)} %get-tuple-element.7), channel_id=1, source_target_pairs={{0,1},{1,2},{2,3},{3,4},{4,5},{5,6},{6,7},{7,8},{8,9},{9,10},{10,1... | collective-permute-start | bytes 368648 | tf_op jit(solution)/shard_map/ppermute | solution.py:19
  109.7 1.9 collective-permute-start.1
  111.7 1.0 stack.134
  112.6 7.0 %collective-permute-done.1 = bf16[8,16,1,480]{3,1,2,0:T(8,128)(2,1)S(1)} collective-permute-done((bf16[8,16,1,480]{3,1,2,0:T(8,128)(2,1)S(1)}, bf16[8,16,1,480]{3,1,2,0:T(8,128)(2,1)S(1)}, u32[]{:S(2)}, u32[]{:S(2)}) %collective-permute-start.1) | collective-permute-done | bytes 122912 | tf_op jit(solution)/shard_map/ppermute | solution.py:21
  121.4 1.2 fusion.11
  123.1 1.0 reshape.40
  124.5 2.8 %reshape.56 = bf16[32,2,3840]{2,1,0:T(2,128)(2,1)S(1)} reshape(bf16[32,8,16,60]{3,2,1,0:T(8,128)(2,1)S(1)} %bitcast.334) | data formatting | bytes 983040
  127.4 30.0 %all_to_all.61 = bf16[32,2,3840]{2,1,0:T(2,128)(2,1)S(1)} all-to-all(bf16[32,2,3840]{2,1,0:T(2,128)(2,1)S(1)} %reshape.56), channel_id=1, replica_groups=mesh['off'=32,'rows'=16] {'off'}, dimensions={0} | all-to-all | bytes 983040 | tf_op jit(solution)/shard_map/all_to_all | solution.py:44
  157.4 3.5 %reshape.57 = bf16[32,8,16,60]{3,2,1,0:T(8,128)(2,1)S(1)} reshape(bf16[32,2,3840]{2,1,0:T(2,128)(2,1)S(1)} %all_to_all.61) | data formatting | bytes 983040
  163.9 1.4 fusion.1
  165.3 2.8 %reshape.58 = bf16[32,2,3840]{2,1,0:T(2,128)(2,1)S(1)} reshape(bf16[256,1,16,60]{3,2,1,0:T(8,128)(2,1)S(1)} %bitcast.337) | data formatting | bytes 983040
  168.1 33.1 %all_to_all.62 = bf16[32,2,3840]{2,1,0:T(2,128)(2,1)S(1)} all-to-all(bf16[32,2,3840]{2,1,0:T(2,128)(2,1)S(1)} %reshape.58), channel_id=1, replica_groups=mesh['off'=32,'rows'=16] {'off'}, dimensions={0} | all-to-all | bytes 983040 | tf_op jit(solution)/shard_map/all_to_all | solution.py:46
  201.2 3.5 %reshape.59 = bf16[256,1,16,60]{3,2,1,0:T(8,128)(2,1)S(1)} reshape(bf16[32,2,3840]{2,1,0:T(2,128)(2,1)S(1)} %all_to_all.62) | data formatting | bytes 983040
  204.8 0.7 copy.154
  205.5 0.9 reshape.43
  206.6 5.6 %collective-permute-start.2 = (bf16[8,16,1,480]{3,1,2,0:T(8,128)(2,1)S(1)}, bf16[8,16,1,480]{3,1,2,0:T(8,128)(2,1)S(1)}, u32[]{:S(2)}, u32[]{:S(2)}) collective-permute-start(bf16[8,16,1,480]{3,1,2,0:T(8,128)(2,1)S(1)} %get-tuple-element.5), channel_id=1, source_target_pairs={{0,1},{1,2},{2,3},{3,4},{4,5},{5,6},{6,7},{7,8},{8,9},{9,10},{10,1... | collective-permute-start | bytes 368648 | tf_op jit(solution)/shard_map/ppermute | solution.py:19
  212.2 1.9 collective-permute-start.3
  214.1 1.0 stack.154
  215.1 7.0 %collective-permute-done.3 = bf16[8,16,1,480]{3,1,2,0:T(8,128)(2,1)S(1)} collective-permute-done((bf16[8,16,1,480]{3,1,2,0:T(8,128)(2,1)S(1)}, bf16[8,16,1,480]{3,1,2,0:T(8,128)(2,1)S(1)}, u32[]{:S(2)}, u32[]{:S(2)}) %collective-permute-start.3) | collective-permute-done | bytes 122912 | tf_op jit(solution)/shard_map/ppermute | solution.py:21
  223.9 1.2 fusion.12
  225.1 1.2 copy.167
  (57 shorter events, 10.8 us)
Async XLA Ops:
  0.0 22.3 %copy-start.1 = (f32[2,16]{1,0:T(2,128)S(1)}, f32[2,16]{1,0:T(2,128)}, u32[]{:S(2)}) copy-start(f32[2,16]{1,0:T(2,128)} %param.7) | copy-start | bytes 388
  6.1 45.5 %all-to-all-start = ((bf16[32,2,3840]{2,1,0:T(2,128)(2,1)}), bf16[32,2,3840]{2,1,0:T(2,128)(2,1)S(1)}, u32[]{:S(2)}, u32[]{:S(2)}) async-start(bf16[32,2,3840]{2,1,0:T(2,128)(2,1)} %reshape.52), calls=%async_computation | async-start | bytes 983040 | tf_op jit(solution)/shard_map/all_to_all | solution.py:44
  56.7 1.4 copy-start.3
  59.6 52.0 %copy-start.2 = (f32[2,16]{1,0:T(2,128)S(1)}, f32[2,16]{1,0:T(2,128)}, u32[]{:S(2)}) copy-start(f32[2,16]{1,0:T(2,128)} %param.9) | copy-start | bytes 388
  103.2 9.4 %collective-permute-start = (bf16[8,16,1,480]{3,1,2,0:T(8,128)(2,1)S(1)}, bf16[8,16,1,480]{3,1,2,0:T(8,128)(2,1)S(1)}, u32[]{:S(2)}, u32[]{:S(2)}) collective-permute-start(bf16[8,16,1,480]{3,1,2,0:T(8,128)(2,1)S(1)} %get-tuple-element.7), channel_id=1, source_target_pairs={{0,1},{1,2},{2,3},{3,4},{4,5},{5,6},{6,7},{7,8},{8,9},{9,10},{10,1... | collective-permute-start | bytes 368648 | tf_op jit(solution)/shard_map/ppermute | solution.py:19
  109.7 9.9 %collective-permute-start.1 = (bf16[8,16,1,480]{3,1,2,0:T(8,128)(2,1)S(1)}, bf16[8,16,1,480]{3,1,2,0:T(8,128)(2,1)S(1)}, u32[]{:S(2)}, u32[]{:S(2)}) collective-permute-start(bf16[8,16,1,480]{3,1,2,0:T(8,128)(2,1)S(1)} %get-tuple-element.8), channel_id=1, source_target_pairs={{1,0},{2,1},{3,2},{4,3},{5,4},{6,5},{7,6},{8,7},{9,8},{10,9},{11,1... | collective-permute-start | bytes 368648 | tf_op jit(solution)/shard_map/ppermute | solution.py:21
  120.1 1.4 copy-start
  206.6 8.5 %collective-permute-start.2 = (bf16[8,16,1,480]{3,1,2,0:T(8,128)(2,1)S(1)}, bf16[8,16,1,480]{3,1,2,0:T(8,128)(2,1)S(1)}, u32[]{:S(2)}, u32[]{:S(2)}) collective-permute-start(bf16[8,16,1,480]{3,1,2,0:T(8,128)(2,1)S(1)} %get-tuple-element.5), channel_id=1, source_target_pairs={{0,1},{1,2},{2,3},{3,4},{4,5},{5,6},{6,7},{7,8},{8,9},{9,10},{10,1... | collective-permute-start | bytes 368648 | tf_op jit(solution)/shard_map/ppermute | solution.py:19
  212.2 9.9 %collective-permute-start.3 = (bf16[8,16,1,480]{3,1,2,0:T(8,128)(2,1)S(1)}, bf16[8,16,1,480]{3,1,2,0:T(8,128)(2,1)S(1)}, u32[]{:S(2)}, u32[]{:S(2)}) collective-permute-start(bf16[8,16,1,480]{3,1,2,0:T(8,128)(2,1)S(1)} %get-tuple-element.6), channel_id=1, source_target_pairs={{1,0},{2,1},{3,2},{4,3},{5,4},{6,5},{7,6},{8,7},{9,8},{10,9},{11,1... | collective-permute-start | bytes 368648 | tf_op jit(solution)/shard_map/ppermute | solution.py:21
where the time goes:
time: 231 us; the launch traced here: 227 us
  blocking collectives  98.6 us (43%)
  local copies, waits for them, and re-layouts  45.3 us (20%)
  waiting for transfers between devices  43.4 us (19%)
  starting transfers between devices  32.1 us (14%)
  matrix products  5.28 us (2%)
    all_to_all x2, blocking collectives, swapped_mix(): lax.all_to_all(mixed, 'off', split_axis=0, concat_axis=2, tiled=True)  68.6 us
    unnamed x44, local copies, waits for them, and re-layouts  32.9 us
    all_to_all x1, blocking collectives, swapped_mix(): lax.all_to_all(split_view, 'off', split_axis=2, concat_axis=0, tiled=True)  30 us
    all_to_all x1, waiting for transfers between devices, swapped_mix(): lax.all_to_all(split_view, 'off', split_axis=2, concat_axis=0, tiled=True)  29.4 us
    all_to_all x1, starting transfers between devices, swapped_mix(): lax.all_to_all(split_view, 'off', split_axis=2, concat_axis=0, tiled=True)  16.1 us
    ppermute x2, waiting for transfers between devices, with_halo(): lax.ppermute(head, axis, [((i + 1) % count, i) for i in range(ends)])  14 us
    ppermute x2, starting transfers between devices, with_halo(): lax.ppermute(tail, axis, [(i, (i + 1) % count) for i in range(ends)])  12.1 us
  transfers between devices with their start and end apart: 5, of which 3 were waited for; matrix products, arithmetic and copies ran while one was open for 1% of the time, Pallas kernels for 0%

commit v1 on v0

v1 whole, which is shorter than its diff:
```python
import jax
import jax.numpy as jnp
from jax import lax
from jax.experimental import pallas as pl
from jax.experimental.pallas import tpu as pltpu
from jax.sharding import PartitionSpec as P

MESH = pl.DeviceIdType.MESH
CH = 16
ROUNDS = 2
HALF = 8
BLOCK = HALF * CH
ROWS = 4
WIDTH = 480
LANES = 512
OWN = BLOCK
EDGE = 3 * BLOCK
DEPTH = 512
ORDER = (0, 3, 1, 2)


def kernel(n_off, n_rows, x_ref, ok_ref, ob_ref, sk_ref, sb_ref, o_ref,
           xb, mixed, w_off, w_sp, bias, ss, rs, hs, hr):
    i, r = lax.axis_index("off"), lax.axis_index("rows")
    odd = lax.rem(i, 2)
    s = 1 - 2 * odd

    def inside(t):
        return (t >= 0) & (t < n_off)

    def row_inside(t):
        return (t >= 0) & (t < n_rows)

    barrier = pltpu.get_barrier_semaphore()
    count = jnp.int32(0)
    offs = (i - 2, i + 2, i + s, i - s, i + 3 * s)
    for t in offs:
        @pl.when(inside(t))
        def _():
            pl.semaphore_signal(barrier, inc=1, device_id=(t, r), device_id_type=MESH)
        count = count + inside(t).astype(jnp.int32)
    for t in (r - 1, r + 1):
        @pl.when(row_inside(t))
        def _():
            pl.semaphore_signal(barrier, inc=1, device_id=(i, t), device_id_type=MESH)
        count = count + row_inside(t).astype(jnp.int32)
    pl.semaphore_wait(barrier, count)

    edge_src = pl.multiple_of(OWN + (HALF - 1) * CH * (1 - odd), CH)
    near = pl.multiple_of(EDGE + 2 * CH * (1 - odd), CH)
    far = pl.multiple_of(EDGE + 2 * CH * odd, CH)

    def flows(rnd, y):
        own = pl.ds(OWN, BLOCK)
        edge = pl.ds(edge_src, CH)
        table = (
            (own, pl.ds(0, BLOCK), i + 2, i - 2),
            (own, pl.ds(2 * BLOCK, BLOCK), i - 2, i + 2),
            (edge, pl.ds(EDGE + CH, CH), i + s, i + s),
            (edge, pl.ds(near, CH), i - s, i - s),
            (edge, pl.ds(far, CH), i + 3 * s, i + 3 * s),
        )
        for f, (src, dst, to, come) in enumerate(table):
            copy = pltpu.make_async_remote_copy(
                src_ref=xb.at[rnd, y, src, :], dst_ref=xb.at[rnd, y, dst, :],
                send_sem=ss.at[rnd, y, f], recv_sem=rs.at[rnd, y, f],
                device_id=(to, r), device_id_type=MESH)
            yield copy, inside(to), inside(come)

    def send(rnd, y):
        for copy, to, _ in flows(rnd, y):
            @pl.when(to)
            def _():
                copy.start()

    def receive(rnd, y):
        for copy, _, come in flows(rnd, y):
            @pl.when(come)
            def _():
                copy.wait_recv()

    def sent(rnd, y):
        for copy, to, _ in flows(rnd, y):
            @pl.when(to)
            def _():
                copy.wait_send()

    def halo(rnd, side):
        src, dst, to, come = ((1, ROWS + 1, r - 1, r + 1), (ROWS, 0, r + 1, r - 1))[side]
        copy = pltpu.make_async_remote_copy(
            src_ref=mixed.at[rnd, pl.ds(src * BLOCK, BLOCK), :],
            dst_ref=mixed.at[rnd, pl.ds(dst * BLOCK, BLOCK), :],
            send_sem=hs.at[rnd, side], recv_sem=hr.at[rnd, side],
            device_id=(i, to), device_id_type=MESH)
        return copy, row_inside(to), row_inside(come)

    for y in range(ROWS):
        xb[0, y, OWN:OWN + BLOCK, :] = x_ref[y]
    for y in ORDER:
        send(0, y)

    xb[:, :, EDGE + 3 * CH:DEPTH, :] = jnp.zeros((ROUNDS, ROWS, DEPTH - EDGE - 3 * CH, LANES), jnp.bfloat16)

    @pl.when(i < 2)
    def _():
        xb[:, :, 0:BLOCK, :] = jnp.zeros((ROUNDS, ROWS, BLOCK, LANES), jnp.bfloat16)
        xb[:, :, EDGE:EDGE + CH, :] = jnp.zeros((ROUNDS, ROWS, CH, LANES), jnp.bfloat16)

    @pl.when(i >= n_off - 2)
    def _():
        xb[:, :, 2 * BLOCK:3 * BLOCK, :] = jnp.zeros((ROUNDS, ROWS, BLOCK, LANES), jnp.bfloat16)
        xb[:, :, EDGE + 2 * CH:EDGE + 3 * CH, :] = jnp.zeros((ROUNDS, ROWS, CH, LANES), jnp.bfloat16)

    @pl.when(r == 0)
    def _():
        mixed[:, 0:BLOCK, :] = jnp.zeros((ROUNDS, BLOCK, LANES), jnp.bfloat16)

    @pl.when(r == n_rows - 1)
    def _():
        mixed[:, (ROWS + 1) * BLOCK:, :] = jnp.zeros((ROUNDS, BLOCK, LANES), jnp.bfloat16)

    row = lax.broadcasted_iota(jnp.int32, (BLOCK, BLOCK), 0)
    col = lax.broadcasted_iota(jnp.int32, (BLOCK, BLOCK), 1)
    v_out, v_in = row // CH, col // CH
    spread = (lax.broadcasted_iota(jnp.int32, (CH, BLOCK), 1) % CH
              == lax.broadcasted_iota(jnp.int32, (CH, BLOCK), 0)).astype(jnp.bfloat16)
    pick = (lax.broadcasted_iota(jnp.int32, (BLOCK, CH), 0) % CH
            == lax.broadcasted_iota(jnp.int32, (BLOCK, CH), 1))
    edge_row = (HALF - 1) * (1 - odd)
    for rnd in range(ROUNDS):
        for kind, (k_ref, b_ref) in enumerate(((ok_ref, ob_ref), (sk_ref, sb_ref))):
            bias[rnd, kind] = jnp.sum(jnp.where(pick, b_ref[rnd:rnd + 1, :], 0.0), axis=1, keepdims=True)
            wide = jnp.dot(k_ref[rnd], spread, preferred_element_type=jnp.float32)
            taps = [jnp.concatenate([wide[t * CH:(t + 1) * CH]] * HALF, axis=0) for t in range(9)]
            if kind == 0:
                edges = jnp.zeros((BLOCK, BLOCK), jnp.float32)
                for a in range(3):
                    block = jnp.zeros((BLOCK, BLOCK), jnp.float32)
                    for b in range(3):
                        block = jnp.where(v_in - v_out == b - 1, taps[3 * a + b], block)
                    w_off[rnd, :, a * BLOCK:(a + 1) * BLOCK] = block.astype(jnp.bfloat16)
                    outer = jnp.where(odd == 1, taps[3 * a], taps[3 * a + 2])
                    edges = jnp.where((v_in == a) & (v_out == edge_row), outer, edges)
                w_off[rnd, :, EDGE:DEPTH] = edges.astype(jnp.bfloat16)
            else:
                for a in range(3):
                    for b in range(3):
                        block = jnp.where(v_in == v_out, taps[3 * a + b], 0.0)
                        w_sp[rnd, b * BLOCK:(b + 1) * BLOCK, a * BLOCK:(a + 1) * BLOCK] = block.astype(jnp.bfloat16)

    image = lax.broadcasted_iota(jnp.int32, (BLOCK, LANES), 1) < WIDTH

    def mix(rnd, y):
        total = jnp.dot(w_off[rnd], xb[rnd, y], preferred_element_type=jnp.float32) + bias[rnd, 0]
        value = jnp.where(image, jnp.maximum(total, 0.0), 0.0)
        mixed[rnd, (y + 1) * BLOCK:(y + 2) * BLOCK, :] = value.astype(jnp.bfloat16)

    def spatial(rnd, y):
        parts = jnp.dot(w_sp[rnd], mixed[rnd, y * BLOCK:(y + 3) * BLOCK, :], preferred_element_type=jnp.float32)
        total = (pltpu.roll(parts[:BLOCK], 1, 1) + parts[BLOCK:2 * BLOCK]
                 + pltpu.roll(parts[2 * BLOCK:], LANES - 1, 1) + bias[rnd, 1])
        value = jnp.maximum(total, 0.0).astype(jnp.bfloat16)
        if rnd == 0:
            xb[1, y, OWN:OWN + BLOCK, :] = value
            send(1, y)
        else:
            o_ref[y] = value

    for rnd in range(ROUNDS):
        for y in ORDER:
            receive(rnd, y)
            mix(rnd, y)
            if y in (0, 3):
                copy, to, _ = halo(rnd, 0 if y == 0 else 1)

                @pl.when(to)
                def _():
                    copy.start()
            if y == 1:
                copy, _, come = halo(rnd, 1)

                @pl.when(come)
                def _():
                    copy.wait_recv()
                spatial(rnd, 0)
            if y == 2:
                copy, _, come = halo(rnd, 0)

                @pl.when(come)
                def _():
                    copy.wait_recv()
                for z in (3, 1, 2):
                    spatial(rnd, z)

    for rnd in range(ROUNDS):
        for y in range(ROWS):
            sent(rnd, y)
        for side in range(2):
            copy, to, _ = halo(rnd, side)

            @pl.when(to)
            def _():
                copy.wait_send()


def local(volume, offset_kernels, offset_biases, spatial_kernels, spatial_biases):
    n_off, n_rows = lax.axis_size("off"), lax.axis_size("rows")
    x = jnp.transpose(volume, (2, 0, 1, 3)).reshape(ROWS, BLOCK, WIDTH)
    x = jnp.pad(x, ((0, 0), (0, 0), (0, LANES - WIDTH)))
    vmem = pl.BlockSpec(memory_space=pltpu.VMEM)
    out = pl.pallas_call(
        lambda *refs: kernel(n_off, n_rows, *refs),
        out_shape=jax.ShapeDtypeStruct((ROWS, BLOCK, LANES), jnp.bfloat16),
        in_specs=[vmem] * 5,
        out_specs=vmem,
        scratch_shapes=[
            pltpu.VMEM((ROUNDS, ROWS, DEPTH, LANES), jnp.bfloat16),
            pltpu.VMEM((ROUNDS, (ROWS + 2) * BLOCK, LANES), jnp.bfloat16),
            pltpu.VMEM((ROUNDS, BLOCK, DEPTH), jnp.bfloat16),
            pltpu.VMEM((ROUNDS, 3 * BLOCK, 3 * BLOCK), jnp.bfloat16),
            pltpu.VMEM((ROUNDS, 2, BLOCK, 1), jnp.float32),
            pltpu.SemaphoreType.DMA((ROUNDS, ROWS, 5)),
            pltpu.SemaphoreType.DMA((ROUNDS, ROWS, 5)),
            pltpu.SemaphoreType.DMA((ROUNDS, 2)),
            pltpu.SemaphoreType.DMA((ROUNDS, 2)),
        ],
        compiler_params=pltpu.CompilerParams(collective_id=0, has_side_effects=True, vmem_limit_bytes=40 << 20),
        cost_estimate=pl.CostEstimate(flops=1 << 30, bytes_accessed=1 << 20, transcendentals=0),
        name="filter_rounds",
    )(x, offset_kernels.reshape(ROUNDS, 9 * CH, CH), offset_biases,
      spatial_kernels.reshape(ROUNDS, 9 * CH, CH), spatial_biases)
    out = out[:, :, :WIDTH].reshape(ROWS, HALF, CH, WIDTH)
    return jnp.transpose(out, (1, 2, 0, 3))


def solution(mesh):
    in_specs = (P("off", None, "rows", None), P(), P(), P(), P())
    out_specs = P("off", None, "rows", None)
    return jax.shard_map(local, mesh=mesh, in_specs=in_specs, out_specs=out_specs, check_vma=False)
```

time: 231 us -> 72.6 us (0.31)
  the two profiles are of different devices: /device:TPU:57 before, /device:TPU:6 now
where the time goes in v1:
time: 72.6 us; the launch traced here: 71.9 us
  Pallas kernels  68.6 us (94%)
  local copies, waits for them, and re-layouts  3.24 us (4%)
    pallas_call x1, Pallas kernels, local(): pl.pallas_call(lambda *refs: kernel(n_off, n_rows, *refs), out_shape=jax....  68.6 us

profile of v1, /device:TPU:6, one launch (start us, length us, event | category | flops | bytes accessed | tf_op | source)
XLA Modules:
  0.0 71.9 jit_solution(14742642817455764184)
XLA Ops:
  0.0 1.1 %copy.6 = bf16[4,8,16,480]{3,2,1,0:T(8,128)(2,1)S(1)} copy(bf16[4,8,16,480]{3,0,2,1:T(4,128)(2,1)} %bitcast.13) | data formatting | bytes 983040 | tf_op jit(solution)/shard_map/transpose | solution.py:208
  1.1 0.0 copy-start
  1.2 0.0 copy-start.1
  1.2 0.0 copy-start.2
  1.2 0.0 copy-start.3
  1.2 0.1 pad.4.refs_0_
  1.3 0.8 %copy-done = bf16[2,9,16,16]{3,2,1,0:T(8,128)(2,1)S(1)} copy-done((bf16[2,9,16,16]{3,2,1,0:T(8,128)(2,1)S(1)}, bf16[2,9,16,16]{3,2,1,0:T(8,128)(2,1)}, u32[]{:S(2)}) %copy-start) | copy-done | bytes 9240
  2.0 0.0 copy-done.1
  2.1 0.0 copy-done.2
  2.1 0.0 copy-done.3
  2.1 68.6 %filter_rounds.1 = bf16[4,128,512]{2,1,0:T(8,128)(2,1)S(1)} custom-call(bf16[4,128,512]{2,1,0:T(8,128)(2,1)S(1)} %pad.4.refs_0_, bf16[2,144,16]{2,1,0:T(8,128)(2,1)S(1)} %bitcast.10, f32[2,16]{1,0:T(2,128)S(1)} %copy-done.2, bf16[2,144,16]{2,1,0:T(8,128)(2,1)S(1)} %bitcast.11, f32[2,16]{1,0:T(2,128)S(1)} %copy-done.3), custom_call_target="tpu_custom_call" | custom-call | flops 1073741824 | bytes 1048576 | tf_op jit(solution)/shard_map/filter_rounds/pallas_call | solution.py:211
  70.7 1.2 %copy.9 = bf16[4,8,16,480]{3,0,2,1:T(4,128)(2,1)} copy(bf16[4,8,16,480]{3,2,1,0:T(8,128)(2,1)S(1)} %bitcast.9) | data formatting | bytes 983040 | tf_op jit(solution)/shard_map/reshape | solution.py:232
Async XLA Ops:
  1.1 0.9 %copy-start = (bf16[2,9,16,16]{3,2,1,0:T(8,128)(2,1)S(1)}, bf16[2,9,16,16]{3,2,1,0:T(8,128)(2,1)}, u32[]{:S(2)}) copy-start(bf16[2,9,16,16]{3,2,1,0:T(8,128)(2,1)} %param.6) | copy-start | bytes 27652
  1.2 0.9 %copy-start.1 = (bf16[2,9,16,16]{3,2,1,0:T(8,128)(2,1)S(1)}, bf16[2,9,16,16]{3,2,1,0:T(8,128)(2,1)}, u32[]{:S(2)}) copy-start(bf16[2,9,16,16]{3,2,1,0:T(8,128)(2,1)} %param.8) | copy-start | bytes 27652
  1.2 0.9 %copy-start.2 = (f32[2,16]{1,0:T(2,128)S(1)}, f32[2,16]{1,0:T(2,128)}, u32[]{:S(2)}) copy-start(f32[2,16]{1,0:T(2,128)} %refs_2_.1) | copy-start | bytes 388
  1.2 0.9 %copy-start.3 = (f32[2,16]{1,0:T(2,128)S(1)}, f32[2,16]{1,0:T(2,128)}, u32[]{:S(2)}) copy-start(f32[2,16]{1,0:T(2,128)} %refs_4_.1) | copy-start | bytes 388

commit v2 on v1

v2 whole, which is shorter than its diff:
```python
import jax
import jax.numpy as jnp
from jax import lax
from jax.experimental import pallas as pl
from jax.experimental.pallas import tpu as pltpu
from jax.sharding import PartitionSpec as P

MESH = pl.DeviceIdType.MESH
CH = 16
ROUNDS = 2
HALF = 8
BLOCK = HALF * CH
INNER = BLOCK - CH
ROWS = 4
WIDTH = 480
LANES = 512
WHOLE = 384
REST = 96
QUARTER = BLOCK - REST
OWN = BLOCK
ORDER = (0, 3, 1, 2)
FIRST = 3


def kernel(n_off, n_rows, x_hbm, ok_hbm, ob_hbm, sk_hbm, sb_hbm, o_ref,
           x_ref, ok_ref, ob_ref, sk_ref, sb_ref, ls,
           xb, mixed, packed, part_out, part_in, held, side_in, w_off, w_sp, bias,
           ss, rs, ps, pr, es, er, hs, hr):
    i, r = lax.axis_index("off"), lax.axis_index("rows")
    odd = lax.rem(i, 2)
    s = 1 - 2 * odd
    pair = i + s

    def inside(t):
        return (t >= 0) & (t < n_off)

    def row_inside(t):
        return (t >= 0) & (t < n_rows)

    loads = [pltpu.make_async_copy(a, b, ls.at[n]) for n, (a, b) in enumerate(
        ((x_hbm, x_ref), (ok_hbm, ok_ref), (ob_hbm, ob_ref), (sk_hbm, sk_ref), (sb_hbm, sb_ref)))]
    for load in loads:
        load.start()

    barrier = pltpu.get_barrier_semaphore()
    count = jnp.int32(1)
    pl.semaphore_signal(barrier, inc=1, device_id=(pair, r), device_id_type=MESH)
    for t in (i - 2, i + 2):
        @pl.when(inside(t))
        def _():
            pl.semaphore_signal(barrier, inc=1, device_id=(t, r), device_id_type=MESH)
        count = count + inside(t).astype(jnp.int32)
    for t in (r - 1, r + 1):
        @pl.when(row_inside(t))
        def _():
            pl.semaphore_signal(barrier, inc=1, device_id=(i, t), device_id_type=MESH)
        count = count + row_inside(t).astype(jnp.int32)

    def plane_at(p):
        return pl.multiple_of(CH * (p + odd * (HALF - 1 - 2 * p)), CH)

    lane = lax.broadcasted_iota(jnp.int32, (QUARTER, BLOCK), 1)

    def pack(rnd, y):
        n = QUARTER if rnd == 0 else CH
        last = xb[rnd, y, OWN + REST:OWN + REST + n, WHOLE:].astype(jnp.float32)
        for g in range(3):
            at = g * QUARTER
            keep = xb[rnd, y, OWN + at:OWN + at + n, WHOLE:]
            moved = pltpu.roll(last, REST - at, 1).astype(jnp.bfloat16)
            packed[rnd, y, at:at + n, :] = jnp.where(lane[:n] < REST, keep, moved)
            if n < QUARTER:
                packed[rnd, y, at + n:at + QUARTER, :] = xb[rnd, y, OWN + at + n:OWN + at + QUARTER, WHOLE:]

    def unpack(rnd, y, base):
        n = QUARTER if rnd == 0 else CH
        value = None
        for g in (2, 1, 0):
            at = base + g * QUARTER
            moved = pltpu.roll(xb[rnd, y, at:at + n, WHOLE:].astype(jnp.float32), (g + 1) * QUARTER, 1)
            value = moved if value is None else jnp.where(lane[:n] < (g + 1) * QUARTER, moved, value)
        xb[rnd, y, base + REST:base + REST + n, WHOLE:] = value.astype(jnp.bfloat16)

    sides = ((0, i + 2, i - 2), (2 * BLOCK, i - 2, i + 2))

    def flows(rnd, y):
        n = BLOCK if rnd == 0 else INNER
        for f, (at, to, come) in enumerate(sides):
            yield pltpu.make_async_remote_copy(
                src_ref=xb.at[rnd, y, pl.ds(OWN, n), pl.ds(0, WHOLE)],
                dst_ref=xb.at[rnd, y, pl.ds(at, n), pl.ds(0, WHOLE)],
                send_sem=ss.at[rnd, y, 2 * f], recv_sem=rs.at[rnd, y, 2 * f],
                device_id=(to, r), device_id_type=MESH), inside(to), inside(come)
            yield pltpu.make_async_remote_copy(
                src_ref=packed.at[rnd, y],
                dst_ref=xb.at[rnd, y, pl.ds(at, REST), pl.ds(WHOLE, BLOCK)],
                send_sem=ss.at[rnd, y, 2 * f + 1], recv_sem=rs.at[rnd, y, 2 * f + 1],
                device_id=(to, r), device_id_type=MESH), inside(to), inside(come)

    def edge_flows():
        for f, (at, to, come) in enumerate(sides):
            yield pltpu.make_async_remote_copy(
                src_ref=xb.at[1, :, pl.ds(OWN + INNER, CH)],
                dst_ref=xb.at[1, :, pl.ds(at + INNER, CH)],
                send_sem=es.at[f], recv_sem=er.at[f],
                device_id=(to, r), device_id_type=MESH), inside(to), inside(come)

    def start(copies):
        for copy, to, _ in copies:
            @pl.when(to)
            def _():
                copy.start()

    def sent(copies):
        for copy, to, _ in copies:
            @pl.when(to)
            def _():
                copy.wait_send()

    def arrived(copies):
        for copy, _, come in copies:
            @pl.when(come)
            def _():
                copy.wait_recv()

    def receive(rnd, y):
        arrived(flows(rnd, y))
        for at, _, come in sides:
            @pl.when(inside(come))
            def _():
                unpack(rnd, y, at)

    def partial_copy(rnd, y):
        return pltpu.make_async_remote_copy(
            src_ref=part_out.at[rnd, y], dst_ref=part_in.at[rnd, y],
            send_sem=ps.at[rnd, y], recv_sem=pr.at[rnd, y],
            device_id=(pair, r), device_id_type=MESH)

    def halo(rnd, side, kind):
        src, dst, to, come = ((1, ROWS + 1, r - 1, r + 1), (ROWS, 0, r + 1, r - 1))[side]
        if kind == 0:
            ends = (mixed.at[rnd, pl.ds(src * BLOCK, INNER), :], mixed.at[rnd, pl.ds(dst * BLOCK, INNER), :])
        else:
            ends = (mixed.at[rnd, pl.ds(src * BLOCK + INNER, CH), :], side_in.at[rnd, side])
        return [(pltpu.make_async_remote_copy(
            src_ref=ends[0], dst_ref=ends[1], send_sem=hs.at[rnd, side, kind], recv_sem=hr.at[rnd, side, kind],
            device_id=(i, to), device_id_type=MESH), row_inside(to), row_inside(come))]

    loads[0].wait()
    for y in ORDER:
        for p in range(HALF):
            xb[0, y, OWN + p * CH:OWN + (p + 1) * CH, 0:WIDTH] = x_ref[pl.ds(plane_at(p), CH), y, :]
        pack(0, y)
        if y == ORDER[0]:
            pl.semaphore_wait(barrier, count)
        if y in ORDER[:FIRST]:
            start(flows(0, y))

    for rnd in range(ROUNDS):
        for y in range(ROWS):
            @pl.when(i < 2)
            def _():
                xb[rnd, y, 0:BLOCK, :] = jnp.zeros((BLOCK, LANES), jnp.bfloat16)

            @pl.when(i >= n_off - 2)
            def _():
                xb[rnd, y, 2 * BLOCK:, :] = jnp.zeros((BLOCK, LANES), jnp.bfloat16)

        mixed[rnd, INNER:BLOCK, :] = jnp.zeros((CH, LANES), jnp.bfloat16)
        mixed[rnd, (ROWS + 1) * BLOCK + INNER:, :] = jnp.zeros((CH, LANES), jnp.bfloat16)

        @pl.when(r == 0)
        def _():
            mixed[rnd, 0:INNER, :] = jnp.zeros((INNER, LANES), jnp.bfloat16)

        @pl.when(r == n_rows - 1)
        def _():
            mixed[rnd, (ROWS + 1) * BLOCK:(ROWS + 1) * BLOCK + INNER, :] = jnp.zeros((INNER, LANES), jnp.bfloat16)

    row = lax.broadcasted_iota(jnp.int32, (BLOCK, BLOCK), 0)
    col = lax.broadcasted_iota(jnp.int32, (BLOCK, BLOCK), 1)
    p_out, p_in = row // CH, col // CH
    spread = (lax.broadcasted_iota(jnp.int32, (CH, BLOCK), 1) % CH
              == lax.broadcasted_iota(jnp.int32, (CH, BLOCK), 0)).astype(jnp.bfloat16)
    pick = (lax.broadcasted_iota(jnp.int32, (BLOCK, CH), 0) % CH
            == lax.broadcasted_iota(jnp.int32, (BLOCK, CH), 1))
    for load in loads[1:]:
        load.wait()
    for rnd in range(ROUNDS):
        for kind, (k_ref, b_ref) in enumerate(((ok_ref, ob_ref), (sk_ref, sb_ref))):
            bias[rnd, kind] = jnp.sum(jnp.where(pick, b_ref[rnd:rnd + 1, :], 0.0), axis=1, keepdims=True)
            wide = jnp.dot(k_ref[rnd], spread, preferred_element_type=jnp.float32)
            taps = [wide[t * CH:(t + 1) * CH] for t in range(9)]
            full = [jnp.concatenate([tap] * HALF, axis=0) for tap in taps]
            for a in range(3):
                if kind == 0:
                    block = jnp.zeros((BLOCK, BLOCK), jnp.float32)
                    for b in range(3):
                        block = jnp.where(p_in - p_out == s * (b - 1), full[3 * a + b], block)
                    w_off[rnd, 0:BLOCK, a * BLOCK:(a + 1) * BLOCK] = block.astype(jnp.bfloat16)
                    outer = jnp.where(odd == 1, taps[3 * a + 2], taps[3 * a])
                    outer = jnp.where(p_in[:CH] == HALF - 1, outer, 0.0)
                    w_off[rnd, BLOCK:, a * BLOCK:(a + 1) * BLOCK] = outer.astype(jnp.bfloat16)
                else:
                    for b in range(3):
                        block = jnp.where(p_in == p_out, full[3 * a + b], 0.0)
                        w_sp[rnd, b * BLOCK:(b + 1) * BLOCK, a * BLOCK:(a + 1) * BLOCK] = block.astype(jnp.bfloat16)

    image = lax.broadcasted_iota(jnp.int32, (BLOCK, LANES), 1) < WIDTH

    def mix(rnd, y):
        sums = jnp.dot(w_off[rnd], xb[rnd, y], preferred_element_type=jnp.float32)
        part_out[rnd, y] = sums[BLOCK:].astype(jnp.bfloat16)
        partial_copy(rnd, y).start()
        sums = sums[:BLOCK] + bias[rnd, 0]
        held[y] = sums[INNER:]
        value = jnp.where(image, jnp.maximum(sums, 0.0), 0.0)
        mixed[rnd, (y + 1) * BLOCK:(y + 2) * BLOCK, :] = value.astype(jnp.bfloat16)
        if y in (0, ROWS - 1):
            start(halo(rnd, 0 if y == 0 else 1, 0))

    def mix_last(rnd, y):
        partial_copy(rnd, y).wait_recv()
        sums = held[y] + part_in[rnd, y].astype(jnp.float32)
        value = jnp.where(image[:CH], jnp.maximum(sums, 0.0), 0.0)
        mixed[rnd, (y + 1) * BLOCK + INNER:(y + 2) * BLOCK, :] = value.astype(jnp.bfloat16)
        if y in (0, ROWS - 1):
            start(halo(rnd, 0 if y == 0 else 1, 1))

    def filtered(parts, biases):
        n = parts.shape[0] // 3
        sums = (pltpu.roll(parts[:n], 1, 1) + parts[n:2 * n]
                + pltpu.roll(parts[2 * n:], LANES - 1, 1) + biases)
        return jnp.maximum(sums, 0.0).astype(jnp.bfloat16)

    def spatial(rnd, y):
        parts = jnp.dot(w_sp[rnd], mixed[rnd, y * BLOCK:(y + 3) * BLOCK, :], preferred_element_type=jnp.float32)
        value = filtered(parts, bias[rnd, 1])
        if rnd == 0:
            xb[1, y, OWN:OWN + INNER, :] = value[:INNER]
            pack(1, y)
        else:
            for p in range(HALF - 1):
                o_ref[y, pl.ds(plane_at(p), CH), :] = value[p * CH:(p + 1) * CH]

    def spatial_last(rnd):
        for side in range(2):
            dst = (ROWS + 1, 0)[side]

            @pl.when(row_inside((r + 1, r - 1)[side]))
            def _():
                mixed[rnd, dst * BLOCK + INNER:(dst + 1) * BLOCK, :] = side_in[rnd, side]
        weights = jnp.concatenate([w_sp[rnd, b * BLOCK + INNER:(b + 1) * BLOCK, :] for b in range(3)], axis=0)
        for y in range(ROWS):
            parts = jnp.dot(weights, mixed[rnd, y * BLOCK:(y + 3) * BLOCK, :], preferred_element_type=jnp.float32)
            value = filtered(parts, bias[rnd, 1, INNER:])
            if rnd == 0:
                xb[1, y, OWN + INNER:OWN + BLOCK, :] = value
            else:
                o_ref[y, pl.ds(plane_at(HALF - 1), CH), :] = value

    for rnd in range(ROUNDS):
        for n, y in enumerate(ORDER):
            receive(rnd, y)
            if rnd == 1 and n == 0:
                arrived(edge_flows())
            mix(rnd, y)
            if rnd == 0 and n + FIRST < ROWS:
                start(flows(0, ORDER[n + FIRST]))
            if n == 2:
                arrived(halo(rnd, 1, 0))
                spatial(rnd, 0)
                if rnd == 0:
                    start(flows(1, 0))
            if n == 3:
                arrived(halo(rnd, 0, 0))
                spatial(rnd, 3)
                if rnd == 0:
                    start(flows(1, 3))
                spatial(rnd, 1)
                spatial(rnd, 2)
            if n > 0:
                mix_last(rnd, ORDER[n - 1])
        mix_last(rnd, ORDER[-1])
        for side in range(2):
            arrived(halo(rnd, side, 1))
        spatial_last(rnd)
        if rnd == 0:
            start(edge_flows())
            start(flows(1, 1))
            start(flows(1, 2))

    sent(edge_flows())
    for rnd in range(ROUNDS):
        for y in range(ROWS):
            sent(flows(rnd, y))
            partial_copy(rnd, y).wait_send()
        for side in range(2):
            for kind in range(2):
                sent(halo(rnd, side, kind))


def local(volume, offset_kernels, offset_biases, spatial_kernels, spatial_biases):
    n_off, n_rows = lax.axis_size("off"), lax.axis_size("rows")
    out = pl.pallas_call(
        lambda *refs: kernel(n_off, n_rows, *refs),
        out_shape=jax.ShapeDtypeStruct((ROWS, BLOCK, LANES), jnp.bfloat16),
        in_specs=[pl.BlockSpec(memory_space=pltpu.HBM)] * 5,
        out_specs=pl.BlockSpec(memory_space=pltpu.VMEM),
        scratch_shapes=[
            pltpu.VMEM((BLOCK, ROWS, WIDTH), jnp.bfloat16),
            pltpu.VMEM((ROUNDS, 9 * CH, CH), jnp.bfloat16),
            pltpu.VMEM((ROUNDS, CH), jnp.float32),
            pltpu.VMEM((ROUNDS, 9 * CH, CH), jnp.bfloat16),
            pltpu.VMEM((ROUNDS, CH), jnp.float32),
            pltpu.SemaphoreType.DMA((5,)),
            pltpu.VMEM((ROUNDS, ROWS, 3 * BLOCK, LANES), jnp.bfloat16),
            pltpu.VMEM((ROUNDS, (ROWS + 2) * BLOCK, LANES), jnp.bfloat16),
            pltpu.VMEM((ROUNDS, ROWS, REST, BLOCK), jnp.bfloat16),
            pltpu.VMEM((ROUNDS, ROWS, CH, LANES), jnp.bfloat16),
            pltpu.VMEM((ROUNDS, ROWS, CH, LANES), jnp.bfloat16),
            pltpu.VMEM((ROWS, CH, LANES), jnp.float32),
            pltpu.VMEM((ROUNDS, 2, CH, LANES), jnp.bfloat16),
            pltpu.VMEM((ROUNDS, BLOCK + CH, 3 * BLOCK), jnp.bfloat16),
            pltpu.VMEM((ROUNDS, 3 * BLOCK, 3 * BLOCK), jnp.bfloat16),
            pltpu.VMEM((ROUNDS, 2, BLOCK, 1), jnp.float32),
            pltpu.SemaphoreType.DMA((ROUNDS, ROWS, 4)),
            pltpu.SemaphoreType.DMA((ROUNDS, ROWS, 4)),
            pltpu.SemaphoreType.DMA((ROUNDS, ROWS)),
            pltpu.SemaphoreType.DMA((ROUNDS, ROWS)),
            pltpu.SemaphoreType.DMA((2,)),
            pltpu.SemaphoreType.DMA((2,)),
            pltpu.SemaphoreType.DMA((ROUNDS, 2, 2)),
            pltpu.SemaphoreType.DMA((ROUNDS, 2, 2)),
        ],
        compiler_params=pltpu.CompilerParams(collective_id=0, has_side_effects=True, vmem_limit_bytes=64 << 20),
        cost_estimate=pl.CostEstimate(flops=1 << 30, bytes_accessed=1 << 20, transcendentals=0),
        name="filter_rounds",
    )(volume.reshape(BLOCK, ROWS, WIDTH), offset_kernels.reshape(ROUNDS, 9 * CH, CH), offset_biases,
      spatial_kernels.reshape(ROUNDS, 9 * CH, CH), spatial_biases)
    out = out[:, :, :WIDTH].reshape(ROWS, HALF, CH, WIDTH)
    return jnp.transpose(out, (1, 2, 0, 3))


def solution(mesh):
    in_specs = (P("off", None, "rows", None), P(), P(), P(), P())
    out_specs = P("off", None, "rows", None)
    return jax.shard_map(local, mesh=mesh, in_specs=in_specs, out_specs=out_specs, check_vma=False)
```

time: 72.6 us -> 65.9 us (0.908)
  Pallas kernels: 68.6 us -> 63.1 us
  local copies, waits for them, and re-layouts: 3.24 us -> 2.25 us
    pallas_call x1, Pallas kernels: 68.6 us -> 63.1 us  [local(): pl.pallas_call(lambda *refs: kernel(n_off, n_rows, *refs), out_shape=jax....]
    transpose x1 -> x0, local copies, waits for them, and re-layouts: 1.14 us -> none  [local(): x = jnp.transpose(volume, (2, 0, 1, 3)).reshape(ROWS, BLOCK, WIDTH)]
    reshape x1, local copies, waits for them, and re-layouts: 1.2 us -> 2.25 us  [local(): out = out[:, :, :WIDTH].reshape(ROWS, HALF, CH, WIDTH)]
    unnamed x8 -> x0, local copies, waits for them, and re-layouts: 0.83 us -> none
where the time goes in v2:
time: 65.9 us; the launch traced here: 65.4 us
  Pallas kernels  63.1 us (96%)
  local copies, waits for them, and re-layouts  2.25 us (3%)
    pallas_call x1, Pallas kernels, local(): pl.pallas_call(lambda *refs: kernel(n_off, n_rows, *refs), out_shape=jax....  63.1 us
    reshape x1, local copies, waits for them, and re-layouts, local(): out = out[:, :, :WIDTH].reshape(ROWS, HALF, CH, WIDTH)  2.25 us

profile of v2, /device:TPU:6, one launch (start us, length us, event | category | flops | bytes accessed | tf_op | source)
XLA Modules:
  0.0 65.4 jit_solution(4483823819373524229)
XLA Ops:
  0.0 63.1 %filter_rounds.1 = bf16[4,128,512]{2,1,0:T(8,128)(2,1)} custom-call(bf16[128,4,480]{2,1,0:T(4,128)(2,1)} %bitcast.9, bf16[2,144,16]{2,1,0:T(8,128)(2,1)} %bitcast.10, f32[2,16]{1,0:T(2,128)} %refs_2_.1, bf16[2,144,16]{2,1,0:T(8,128)(2,1)} %bitcast.11, f32[2,16]{1,0:T(2,128)} %refs_4_.1), custom_call_target="tpu_custom_call" | custom-call | flops 1073741824 | bytes 1048576 | tf_op jit(solution)/shard_map/filter_rounds/pallas_call | solution.py:305
  63.1 2.2 %copy.8 = bf16[4,8,16,480]{3,0,2,1:T(4,128)(2,1)} copy(bf16[4,8,16,480]{3,2,1,0:T(8,128)(2,1)} %bitcast.8) | data formatting | bytes 983040 | tf_op jit(solution)/shard_map/reshape | solution.py:341

commit v3 on v2

--- a/solution.py
+++ b/solution.py
@@ -241,7 +241,7 @@
             pack(1, y)
         else:
             for p in range(HALF - 1):
-                o_ref[y, pl.ds(plane_at(p), CH), :] = value[p * CH:(p + 1) * CH]
+                o_ref[pl.ds(plane_at(p), CH), y, :] = value[p * CH:(p + 1) * CH, :WIDTH]
 
     def spatial_last(rnd):
         for side in range(2):
@@ -257,7 +257,7 @@
             if rnd == 0:
                 xb[1, y, OWN + INNER:OWN + BLOCK, :] = value
             else:
-                o_ref[y, pl.ds(plane_at(HALF - 1), CH), :] = value
+                o_ref[pl.ds(plane_at(HALF - 1), CH), y, :] = value[:, :WIDTH]
 
     for rnd in range(ROUNDS):
         for n, y in enumerate(ORDER):
@@ -304,7 +304,7 @@
     n_off, n_rows = lax.axis_size("off"), lax.axis_size("rows")
     out = pl.pallas_call(
         lambda *refs: kernel(n_off, n_rows, *refs),
-        out_shape=jax.ShapeDtypeStruct((ROWS, BLOCK, LANES), jnp.bfloat16),
+        out_shape=pltpu.VMEM((BLOCK, ROWS, WIDTH), jnp.bfloat16),
         in_specs=[pl.BlockSpec(memory_space=pltpu.HBM)] * 5,
         out_specs=pl.BlockSpec(memory_space=pltpu.VMEM),
         scratch_shapes=[
@@ -333,13 +333,13 @@
             pltpu.SemaphoreType.DMA((ROUNDS, 2, 2)),
             pltpu.SemaphoreType.DMA((ROUNDS, 2, 2)),
         ],
-        compiler_params=pltpu.CompilerParams(collective_id=0, has_side_effects=True, vmem_limit_bytes=64 << 20),
+        compiler_params=pltpu.CompilerParams(collective_id=0, has_side_effects=True, vmem_limit_bytes=40 << 20),
         cost_estimate=pl.CostEstimate(flops=1 << 30, bytes_accessed=1 << 20, transcendentals=0),
         name="filter_rounds",
-    )(volume.reshape(BLOCK, ROWS, WIDTH), offset_kernels.reshape(ROUNDS, 9 * CH, CH), offset_biases,
-      spatial_kernels.reshape(ROUNDS, 9 * CH, CH), spatial_biases)
-    out = out[:, :, :WIDTH].reshape(ROWS, HALF, CH, WIDTH)
-    return jnp.transpose(out, (1, 2, 0, 3))
+    )(*[pltpu.with_memory_space_constraint(a, pltpu.HBM) for a in (
+        volume.reshape(BLOCK, ROWS, WIDTH), offset_kernels.reshape(ROUNDS, 9 * CH, CH), offset_biases,
+        spatial_kernels.reshape(ROUNDS, 9 * CH, CH), spatial_biases)])
+    return out.reshape(HALF, CH, ROWS, WIDTH)
 
 
 def solution(mesh):

time: 65.9 us -> 63.7 us (0.967)
  local copies, waits for them, and re-layouts: 2.25 us -> 0.8 us
  Pallas kernels: 63.1 us -> 62.4 us
    reshape x1 -> x0, local copies, waits for them, and re-layouts: 2.25 us -> none  [local(): out = out[:, :, :WIDTH].reshape(ROWS, HALF, CH, WIDTH)]
    unnamed x0 -> x1, local copies, waits for them, and re-layouts: none -> 0.8 us
    pallas_call x1, Pallas kernels: 63.1 us -> 62.4 us  [local(): pl.pallas_call(lambda *refs: kernel(n_off, n_rows, *refs), out_shape=pltp...]
where the time goes in v3:
time: 63.7 us; the launch traced here: 63.2 us
  Pallas kernels  62.4 us (98%)
  local copies, waits for them, and re-layouts  0.8 us (1%)
    pallas_call x1, Pallas kernels, local(): pl.pallas_call(lambda *refs: kernel(n_off, n_rows, *refs), out_shape=pltp...  62.4 us

profile of v3, /device:TPU:6, one launch (start us, length us, event | category | flops | bytes accessed | tf_op | source)
XLA Modules:
  0.0 63.2 jit_solution(4874889504996371669)
XLA Ops:
  0.0 62.4 %filter_rounds.1 = bf16[128,4,480]{2,1,0:T(4,128)(2,1)S(1)} custom-call(bf16[128,4,480]{2,1,0:T(4,128)(2,1)} %bitcast.5, bf16[2,144,16]{2,1,0:T(8,128)(2,1)} %bitcast.6, f32[2,16]{1,0:T(2,128)} %refs_2_.1, bf16[2,144,16]{2,1,0:T(8,128)(2,1)} %bitcast.7, f32[2,16]{1,0:T(2,128)} %refs_4_.1), custom_call_target="tpu_custom_call" | custom-call | flops 1073741824 | bytes 1048576 | tf_op jit(solution)/shard_map/filter_rounds/pallas_call | solution.py:305
  62.4 0.8 %copy.7 = bf16[8,16,4,480]{3,2,1,0:T(4,128)(2,1)} copy(bf16[8,16,4,480]{3,2,1,0:T(4,128)(2,1)S(1)} %bitcast.4) | data formatting | bytes 983040

commit v4 on v3

--- a/solution.py
+++ b/solution.py
@@ -19,13 +19,14 @@
 QUARTER = BLOCK - REST
 OWN = BLOCK
 ORDER = (0, 3, 1, 2)
+LAST = ORDER[-1]
 FIRST = 3
 
 
 def kernel(n_off, n_rows, x_hbm, ok_hbm, ob_hbm, sk_hbm, sb_hbm, o_ref,
            x_ref, ok_ref, ob_ref, sk_ref, sb_ref, ls,
-           xb, mixed, packed, part_out, part_in, held, side_in, w_off, w_sp, bias,
-           ss, rs, ps, pr, es, er, hs, hr):
+           xb, mixed, packed, part_out, part_in, held, side_in, raw_in, w_off, w_sp, w_raw, bias,
+           ss, rs, ps, pr, es, er, hs, hr, ws, wr):
     i, r = lax.axis_index("off"), lax.axis_index("rows")
     odd = lax.rem(i, 2)
     s = 1 - 2 * odd
@@ -45,7 +46,7 @@
     barrier = pltpu.get_barrier_semaphore()
     count = jnp.int32(1)
     pl.semaphore_signal(barrier, inc=1, device_id=(pair, r), device_id_type=MESH)
-    for t in (i - 2, i + 2):
+    for t in (i - 2, i + 2, i - s, i + 3 * s):
         @pl.when(inside(t))
         def _():
             pl.semaphore_signal(barrier, inc=1, device_id=(t, r), device_id_type=MESH)
@@ -105,6 +106,14 @@
                 send_sem=es.at[f], recv_sem=er.at[f],
                 device_id=(to, r), device_id_type=MESH), inside(to), inside(come)
 
+    def raw_flows():
+        for f, (slot, to) in enumerate(((1, pair), (2 * (1 - odd), i - s), (2 * odd, i + 3 * s))):
+            yield pltpu.make_async_remote_copy(
+                src_ref=xb.at[1, LAST, pl.ds(OWN + INNER, CH)],
+                dst_ref=raw_in.at[pl.ds(pl.multiple_of(slot * CH, CH), CH)],
+                send_sem=ws.at[f], recv_sem=wr.at[f],
+                device_id=(to, r), device_id_type=MESH), inside(to), inside(to)
+
     def start(copies):
         for copy, to, _ in copies:
             @pl.when(to)
@@ -165,6 +174,14 @@
             @pl.when(i >= n_off - 2)
             def _():
                 xb[rnd, y, 2 * BLOCK:, :] = jnp.zeros((BLOCK, LANES), jnp.bfloat16)
+
+        @pl.when(i < 2)
+        def _():
+            raw_in[0:CH, :] = jnp.zeros((CH, LANES), jnp.bfloat16)
+
+        @pl.when(i >= n_off - 2)
+        def _():
+            raw_in[2 * CH:, :] = jnp.zeros((CH, LANES), jnp.bfloat16)
 
         mixed[rnd, INNER:BLOCK, :] = jnp.zeros((CH, LANES), jnp.bfloat16)
         mixed[rnd, (ROWS + 1) * BLOCK + INNER:, :] = jnp.zeros((CH, LANES), jnp.bfloat16)
@@ -192,8 +209,11 @@
             wide = jnp.dot(k_ref[rnd], spread, preferred_element_type=jnp.float32)
             taps = [wide[t * CH:(t + 1) * CH] for t in range(9)]
             full = [jnp.concatenate([tap] * HALF, axis=0) for tap in taps]
+            raw = jnp.zeros((CH, BLOCK), jnp.float32)
             for a in range(3):
                 if kind == 0:
+                    theirs = jnp.where(odd == 1, taps[3 * a], taps[3 * a + 2])
+                    raw = jnp.where(p_in[:CH] == a, theirs, raw)
                     block = jnp.zeros((BLOCK, BLOCK), jnp.float32)
                     for b in range(3):
                         block = jnp.where(p_in - p_out == s * (b - 1), full[3 * a + b], block)
@@ -201,6 +221,8 @@
                     outer = jnp.where(odd == 1, taps[3 * a + 2], taps[3 * a])
                     outer = jnp.where(p_in[:CH] == HALF - 1, outer, 0.0)
                     w_off[rnd, BLOCK:, a * BLOCK:(a + 1) * BLOCK] = outer.astype(jnp.bfloat16)
+                    if rnd == 1:
+                        w_raw[...] = raw.astype(jnp.bfloat16)
                 else:
                     for b in range(3):
                         block = jnp.where(p_in == p_out, full[3 * a + b], 0.0)
@@ -210,8 +232,9 @@
 
     def mix(rnd, y):
         sums = jnp.dot(w_off[rnd], xb[rnd, y], preferred_element_type=jnp.float32)
-        part_out[rnd, y] = sums[BLOCK:].astype(jnp.bfloat16)
-        partial_copy(rnd, y).start()
+        if (rnd, y) != (1, LAST):
+            part_out[rnd, y] = sums[BLOCK:].astype(jnp.bfloat16)
+            partial_copy(rnd, y).start()
         sums = sums[:BLOCK] + bias[rnd, 0]
         held[y] = sums[INNER:]
         value = jnp.where(image, jnp.maximum(sums, 0.0), 0.0)
@@ -220,8 +243,12 @@
             start(halo(rnd, 0 if y == 0 else 1, 0))
 
     def mix_last(rnd, y):
-        partial_copy(rnd, y).wait_recv()
-        sums = held[y] + part_in[rnd, y].astype(jnp.float32)
+        if (rnd, y) != (1, LAST):
+            partial_copy(rnd, y).wait_recv()
+            sums = held[y] + part_in[rnd, y].astype(jnp.float32)
+        else:
+            arrived(raw_flows())
+            sums = held[y] + jnp.dot(w_raw[:, 0:3 * CH], raw_in[...], preferred_element_type=jnp.float32)
         value = jnp.where(image[:CH], jnp.maximum(sums, 0.0), 0.0)
         mixed[rnd, (y + 1) * BLOCK + INNER:(y + 2) * BLOCK, :] = value.astype(jnp.bfloat16)
         if y in (0, ROWS - 1):
@@ -287,14 +314,17 @@
         spatial_last(rnd)
         if rnd == 0:
             start(edge_flows())
+            start(raw_flows())
             start(flows(1, 1))
             start(flows(1, 2))
 
     sent(edge_flows())
+    sent(raw_flows())
     for rnd in range(ROUNDS):
         for y in range(ROWS):
             sent(flows(rnd, y))
-            partial_copy(rnd, y).wait_send()
+            if (rnd, y) != (1, LAST):
+                partial_copy(rnd, y).wait_send()
         for side in range(2):
             for kind in range(2):
                 sent(halo(rnd, side, kind))
@@ -321,8 +351,10 @@
             pltpu.VMEM((ROUNDS, ROWS, CH, LANES), jnp.bfloat16),
             pltpu.VMEM((ROWS, CH, LANES), jnp.float32),
             pltpu.VMEM((ROUNDS, 2, CH, LANES), jnp.bfloat16),
+            pltpu.VMEM((3 * CH, LANES), jnp.bfloat16),
             pltpu.VMEM((ROUNDS, BLOCK + CH, 3 * BLOCK), jnp.bfloat16),
             pltpu.VMEM((ROUNDS, 3 * BLOCK, 3 * BLOCK), jnp.bfloat16),
+            pltpu.VMEM((CH, BLOCK), jnp.bfloat16),
             pltpu.VMEM((ROUNDS, 2, BLOCK, 1), jnp.float32),
             pltpu.SemaphoreType.DMA((ROUNDS, ROWS, 4)),
             pltpu.SemaphoreType.DMA((ROUNDS, ROWS, 4)),
@@ -332,6 +364,8 @@
             pltpu.SemaphoreType.DMA((2,)),
             pltpu.SemaphoreType.DMA((ROUNDS, 2, 2)),
             pltpu.SemaphoreType.DMA((ROUNDS, 2, 2)),
+            pltpu.SemaphoreType.DMA((3,)),
+            pltpu.SemaphoreType.DMA((3,)),
         ],
         compiler_params=pltpu.CompilerParams(collective_id=0, has_side_effects=True, vmem_limit_bytes=40 << 20),
         cost_estimate=pl.CostEstimate(flops=1 << 30, bytes_accessed=1 << 20, transcendentals=0),

time: 63.7 us -> 65.7 us (1.031)
  Pallas kernels: 62.4 us -> 64.8 us
    pallas_call x1, Pallas kernels: 62.4 us -> 64.8 us  [local(): pl.pallas_call(lambda *refs: kernel(n_off, n_rows, *refs), out_shape=pltp...]
where the time goes in v4:
time: 65.7 us; the launch traced here: 65.6 us
  Pallas kernels  64.8 us (99%)
  local copies, waits for them, and re-layouts  0.8 us (1%)
    pallas_call x1, Pallas kernels, local(): pl.pallas_call(lambda *refs: kernel(n_off, n_rows, *refs), out_shape=pltp...  64.8 us

profile of v4, /device:TPU:6, one launch (start us, length us, event | category | flops | bytes accessed | tf_op | source)
XLA Modules:
  0.0 65.6 jit_solution(3959504009219770186)
XLA Ops:
  0.0 64.8 %filter_rounds.1 = bf16[128,4,480]{2,1,0:T(4,128)(2,1)S(1)} custom-call(bf16[128,4,480]{2,1,0:T(4,128)(2,1)} %bitcast.5, bf16[2,144,16]{2,1,0:T(8,128)(2,1)} %bitcast.6, f32[2,16]{1,0:T(2,128)} %refs_2_.1, bf16[2,144,16]{2,1,0:T(8,128)(2,1)} %bitcast.7, f32[2,16]{1,0:T(2,128)} %refs_4_.1), custom_call_target="tpu_custom_call" | custom-call | flops 1073741824 | bytes 1048576 | tf_op jit(solution)/shard_map/filter_rounds/pallas_call | solution.py:335
  64.8 0.8 %copy.7 = bf16[8,16,4,480]{3,2,1,0:T(4,128)(2,1)} copy(bf16[8,16,4,480]{3,2,1,0:T(4,128)(2,1)S(1)} %bitcast.4) | data formatting | bytes 983040

commit v5 on v3

--- a/solution.py
+++ b/solution.py
@@ -87,14 +87,14 @@
         n = BLOCK if rnd == 0 else INNER
         for f, (at, to, come) in enumerate(sides):
             yield pltpu.make_async_remote_copy(
+                src_ref=packed.at[rnd, y],
+                dst_ref=xb.at[rnd, y, pl.ds(at, REST), pl.ds(WHOLE, BLOCK)],
+                send_sem=ss.at[rnd, y, 2 * f + 1], recv_sem=rs.at[rnd, y, 2 * f + 1],
+                device_id=(to, r), device_id_type=MESH), inside(to), inside(come)
+            yield pltpu.make_async_remote_copy(
                 src_ref=xb.at[rnd, y, pl.ds(OWN, n), pl.ds(0, WHOLE)],
                 dst_ref=xb.at[rnd, y, pl.ds(at, n), pl.ds(0, WHOLE)],
                 send_sem=ss.at[rnd, y, 2 * f], recv_sem=rs.at[rnd, y, 2 * f],
-                device_id=(to, r), device_id_type=MESH), inside(to), inside(come)
-            yield pltpu.make_async_remote_copy(
-                src_ref=packed.at[rnd, y],
-                dst_ref=xb.at[rnd, y, pl.ds(at, REST), pl.ds(WHOLE, BLOCK)],
-                send_sem=ss.at[rnd, y, 2 * f + 1], recv_sem=rs.at[rnd, y, 2 * f + 1],
                 device_id=(to, r), device_id_type=MESH), inside(to), inside(come)
 
     def edge_flows():

time: 63.7 us -> 63.7 us (level)
  no operation moved by 1% of the time
where the time goes in v5:
time: 63.7 us; the launch traced here: 63.2 us
  Pallas kernels  62.4 us (98%)
  local copies, waits for them, and re-layouts  0.8 us (1%)
    pallas_call x1, Pallas kernels, local(): pl.pallas_call(lambda *refs: kernel(n_off, n_rows, *refs), out_shape=pltp...  62.4 us

profile of v5, /device:TPU:6, one launch (start us, length us, event | category | flops | bytes accessed | tf_op | source)
XLA Modules:
  0.0 63.2 jit_solution(11783938625362943556)
XLA Ops:
  0.0 62.4 %filter_rounds.1 = bf16[128,4,480]{2,1,0:T(4,128)(2,1)S(1)} custom-call(bf16[128,4,480]{2,1,0:T(4,128)(2,1)} %bitcast.5, bf16[2,144,16]{2,1,0:T(8,128)(2,1)} %bitcast.6, f32[2,16]{1,0:T(2,128)} %refs_2_.1, bf16[2,144,16]{2,1,0:T(8,128)(2,1)} %bitcast.7, f32[2,16]{1,0:T(2,128)} %refs_4_.1), custom_call_target="tpu_custom_call" | custom-call | flops 1073741824 | bytes 1048576 | tf_op jit(solution)/shard_map/filter_rounds/pallas_call | solution.py:305
  62.4 0.8 %copy.7 = bf16[8,16,4,480]{3,2,1,0:T(4,128)(2,1)} copy(bf16[8,16,4,480]{3,2,1,0:T(4,128)(2,1)S(1)} %bitcast.4) | data formatting | bytes 983040
